TPU v7x, 32 devices: a whole 2x2x4 slice. The times are simulated.
32 devices in a mesh: seq: 8 (over z, x), fsdp: 4 (over y, core).
Axes of the slice: x: 2, y: 2, z: 4, core: 2. Of those that a mesh axis runs over, the one named last changes fastest.
Arguments:
- tokens: bfloat16 [4, 8192, 768], P('fsdp', 'seq'), may hold values from -6 to 6
- cotangent: bfloat16 [4, 8192, 768], P('fsdp', 'seq'), may hold values from -6 to 6
- starts: int32 [4, 3], P('fsdp'), may hold values from 0 to 7680, as said below
- w_qkv: bfloat16 [768, 2304], P('fsdp'), may hold values from -0.21875 to 0.21875
- w_attn: bfloat16 [768, 768], P('fsdp'), may hold values from -0.625 to 0.625
- w_in: bfloat16 [768, 2304], P('fsdp'), may hold values from -0.21875 to 0.21875
- w_out: bfloat16 [1152, 768], P('fsdp'), may hold values from -0.1875 to 0.1875
- gain_one: bfloat16 [768], P('fsdp'), may hold values from 0.25 to 1.75
- gain_two: bfloat16 [768], P('fsdp'), may hold values from 0.25 to 1.75
Outputs:
- result: bfloat16 [4, 8192, 768], P('fsdp', 'seq')
- grad_tokens: bfloat16 [4, 8192, 768], P('fsdp', 'seq')
- grad_qkv: float32 [768, 2304], P('fsdp')
- grad_attn: float32 [768, 768], P('fsdp')
- grad_in: float32 [768, 2304], P('fsdp')
- grad_out: float32 [1152, 768], P('fsdp')
- grad_gain_one: float32 [768], P('fsdp')
- grad_gain_two: float32 [768], P('fsdp')
Inputs may be any that keep to these rules, and one draw needn't show every extreme that they name: `starts`: row g lists in rising order the first token of each of the 3 sequences of group g: the first is 0 and the last is 7680; the middle one lies either between 256 and 512 or is exactly 7424, so that one sequence of each group reaches from the first token shard to the last.
All inputs are finite; a program needn't handle non-finite values.
Results may differ from a plain program's by a relative error of at most 0.018.
Values may be sent and summed in bfloat16 or wider, within the bound.
A program may use at most 192 MiB of HBM per device.

v0:
```python
import math

import jax
import jax.numpy as jnp
from jax import lax
from jax.sharding import PartitionSpec as P

HEADS = 12
HALF = 64


EPSILON = 1e-05
THETA = 10000.0


def extended(shard, sides, width):
    for axis, dim in sides:
        devices, length = (lax.axis_size(axis), shard.shape[dim])
        up = [(i, (i + 1) % devices) for i in range(devices - 1)]
        down = [(j, i) for i, j in up]
        last = lax.slice_in_dim(shard, length - width, length, axis=dim)
        first = lax.slice_in_dim(shard, 0, width, axis=dim)
        before = lax.ppermute(last, axis, up)
        after = lax.ppermute(first, axis, down)
        shard = jnp.concatenate([before, shard, after], axis=dim)
    return shard


def passed_along(value, axis, steps):
    count = lax.axis_size(axis)
    first, last = (max(0, -steps), min(count, count - steps))
    return lax.ppermute(value, axis, [(source, source + steps) for source in range(first, last)])


def inner_product(left, right):
    return lax.dot_general(
        left, right, (((0,), (0,)), ((), ())), preferred_element_type=jnp.float32
    )


def outer_product(left, right):
    return lax.dot_general(
        left, right, (((1,), (1,)), ((), ())), preferred_element_type=jnp.float32
    )


def norm_parts(values, gain):
    average = jnp.mean(values, -1, keepdims=True)
    centred = values - average
    spread = lax.rsqrt(jnp.mean(centred * centred, -1, keepdims=True) + EPSILON)
    plain = centred * spread
    return (plain, spread, plain * gain)


def norm_back(grad_normed, plain, spread, gain):
    grad_plain = grad_normed * gain
    grad_values = spread * (
        grad_plain
        - jnp.mean(grad_plain, -1, keepdims=True)
        - plain * jnp.mean(grad_plain * plain, -1, keepdims=True)
    )
    return (grad_values, jnp.sum(grad_normed * plain, 0))


def rotate(values, cosine, sine):
    middle = values.shape[-1] // 2
    turned = jnp.concatenate([-values[..., middle:], values[..., :middle]], -1)
    return values * cosine + turned * sine


def rotate_back(grads, cosine, sine):
    middle = grads.shape[-1] // 2
    scaled = grads * sine
    turned = jnp.concatenate([scaled[..., middle:], -scaled[..., :middle]], -1)
    return grads * cosine + turned


def body(tokens, cotangent, starts, w_qkv, w_attn, w_in, w_out, gain_one, gain_two):
    full_qkv, full_attn, full_in, full_out, full_one, full_two = (
        lax.all_gather(w_qkv, "fsdp", axis=0, tiled=True),
        lax.all_gather(w_attn, "fsdp", axis=0, tiled=True),
        lax.all_gather(w_in, "fsdp", axis=0, tiled=True),
        lax.all_gather(w_out, "fsdp", axis=0, tiled=True),
        lax.all_gather(gain_one, "fsdp", axis=0, tiled=True),
        lax.all_gather(gain_two, "fsdp", axis=0, tiled=True),
    )
    first_gain = full_one.astype(jnp.float32)
    second_gain = full_two.astype(jnp.float32)
    inputs = tokens[0].astype(jnp.float32)
    tok_count = inputs.shape[0]
    model_width = inputs.shape[1]
    head_size = model_width // HEADS
    ff_width = full_out.shape[0]
    factor = 1.0 / math.sqrt(head_size)
    seq_index = lax.axis_index("seq")
    group_length = tok_count * lax.axis_size("seq")
    seq_starts = starts[0]
    places = seq_index * tok_count - HALF + jnp.arange(tok_count + 2 * HALF, dtype=jnp.int32)
    before = seq_starts[None, :] <= places[:, None]
    seq_idents = jnp.sum(before.astype(jnp.int32), 1) - 1
    seq_idents = jnp.where(places >= group_length, -2, seq_idents)
    first_token = jnp.max(jnp.where(before, seq_starts[None, :], 0), 1)
    local_idents = seq_idents[HALF : HALF + tok_count]
    position = (places - first_token)[HALF : HALF + tok_count].astype(jnp.float32)
    freqs = THETA ** (-jnp.arange(head_size // 2, dtype=jnp.float32) * 2.0 / head_size)
    angles = position[:, None] * freqs[None, :]
    cosine = jnp.concatenate([jnp.cos(angles), jnp.cos(angles)], -1)[:, None, :]
    sine = jnp.concatenate([jnp.sin(angles), jnp.sin(angles)], -1)[:, None, :]
    plain_one, spread_one, normed = norm_parts(inputs, first_gain)
    normed_low = normed.astype(jnp.bfloat16)
    mixed = jnp.dot(normed_low, full_qkv, preferred_element_type=jnp.float32)
    shape_three = (tok_count, HEADS, head_size)
    query = rotate(mixed[:, :model_width].reshape(shape_three), cosine, sine).astype(jnp.bfloat16)
    key_rot = rotate(
        mixed[:, model_width : 2 * model_width].reshape(shape_three), cosine, sine
    ).astype(jnp.bfloat16)
    value = mixed[:, 2 * model_width :].astype(jnp.bfloat16)
    key_value = jnp.concatenate([key_rot.reshape(tok_count, model_width), value], 1)
    padded = extended(key_value, (("seq", 0),), HALF)
    block = math.gcd(tok_count, 512)
    span = block + 2 * HALF
    offsets = (
        jnp.arange(span, dtype=jnp.int32)[None, :]
        - HALF
        - jnp.arange(block, dtype=jnp.int32)[:, None]
    )
    nearby = jnp.abs(offsets) <= HALF
    beginnings = jnp.arange(tok_count // block, dtype=jnp.int32) * block

    def block_inputs(begin):
        query_block = lax.dynamic_slice_in_dim(query, begin, block, 0)
        pair_block = lax.dynamic_slice_in_dim(padded, begin, span, 0)
        key_block = pair_block[:, :model_width].reshape(span, HEADS, head_size)
        value_block = pair_block[:, model_width:].reshape(span, HEADS, head_size)
        query_ident = lax.dynamic_slice_in_dim(local_idents, begin, block, 0)
        key_ident = lax.dynamic_slice_in_dim(seq_idents, begin, span, 0)
        allowed = nearby & (query_ident[:, None] == key_ident[None, :])
        scores = factor * jnp.einsum(
            "qhd,khd->hqk", query_block, key_block, preferred_element_type=jnp.float32
        )
        return (query_block, key_block, value_block, allowed, scores)

    def forward_block(begin):
        query_block, key_block, value_block, allowed, scores = block_inputs(begin)
        masked = jnp.where(allowed[None], scores, -1e30)
        highest = jnp.max(masked, -1, keepdims=True)
        weights = jnp.where(allowed[None], jnp.exp(masked - highest), 0.0)
        totals = jnp.sum(weights, -1, keepdims=True)
        probs = (weights / totals).astype(jnp.bfloat16)
        context_block = jnp.einsum(
            "hqk,khd->qhd", probs, value_block, preferred_element_type=jnp.float32
        )
        return (context_block.reshape(block, model_width), (highest + jnp.log(totals))[..., 0])

    context_blocks, log_totals = lax.map(forward_block, beginnings)
    context = context_blocks.reshape(tok_count, model_width).astype(jnp.bfloat16)
    hidden = inputs + jnp.dot(context, full_attn, preferred_element_type=jnp.float32)
    plain_two, spread_two, normed_two = norm_parts(hidden, second_gain)
    normed_two_low = normed_two.astype(jnp.bfloat16)
    both = jnp.dot(normed_two_low, full_in, preferred_element_type=jnp.float32)
    gate = both[:, :ff_width]
    upper = both[:, ff_width:]
    active, gelu_back = jax.vjp(lambda entry: jax.nn.gelu(entry, approximate=False), gate)
    act_low = (active * upper).astype(jnp.bfloat16)
    output = hidden + jnp.dot(act_low, full_out, preferred_element_type=jnp.float32)
    grad_result = cotangent[0]
    grad_wout = inner_product(act_low, grad_result)
    grad_act = outer_product(grad_result, full_out)
    grad_gate = gelu_back(grad_act * upper)[0]
    grad_both = jnp.concatenate([grad_gate, grad_act * active], 1).astype(jnp.bfloat16)
    grad_win = inner_product(normed_two_low, grad_both)
    grad_normed_two = outer_product(grad_both, full_in)
    grad_hidden_norm, grad_second = norm_back(grad_normed_two, plain_two, spread_two, second_gain)
    grad_hidden = grad_result.astype(jnp.float32) + grad_hidden_norm
    grad_hidden_low = grad_hidden.astype(jnp.bfloat16)
    grad_wattn = inner_product(context, grad_hidden_low)
    grad_context = outer_product(grad_hidden_low, full_attn).astype(jnp.bfloat16)

    def backward_block(carried, inputs_pair):
        begin, log_total = inputs_pair
        query_block, key_block, value_block, allowed, scores = block_inputs(begin)
        probs = jnp.exp(jnp.where(allowed[None], scores - log_total[..., None], -1e30))
        grad_block = lax.dynamic_slice_in_dim(grad_context, begin, block, 0).reshape(
            block, HEADS, head_size
        )
        grad_probs = jnp.einsum(
            "qhd,khd->hqk", grad_block, value_block, preferred_element_type=jnp.float32
        )
        grad_scores = (
            probs * (grad_probs - jnp.sum(probs * grad_probs, -1, keepdims=True))
        ).astype(jnp.bfloat16)
        grad_query = factor * jnp.einsum(
            "hqk,khd->qhd", grad_scores, key_block, preferred_element_type=jnp.float32
        )
        grad_key = factor * jnp.einsum(
            "hqk,qhd->khd", grad_scores, query_block, preferred_element_type=jnp.float32
        )
        grad_value = jnp.einsum(
            "hqk,qhd->khd",
            probs.astype(jnp.bfloat16),
            grad_block,
            preferred_element_type=jnp.float32,
        )
        grad_pair = jnp.concatenate(
            [grad_key.reshape(span, model_width), grad_value.reshape(span, model_width)], 1
        )
        current = lax.dynamic_slice_in_dim(carried, begin, span, 0)
        carried = lax.dynamic_update_slice_in_dim(carried, current + grad_pair, begin, 0)
        return (carried, grad_query.reshape(block, model_width))

    empty_edges = jnp.zeros((tok_count + 2 * HALF, 2 * model_width), jnp.float32)
    grad_edges, grad_queries = lax.scan(backward_block, empty_edges, (beginnings, log_totals))
    from_lower = passed_along(grad_edges[tok_count + HALF :].astype(jnp.bfloat16), "seq", 1).astype(
        jnp.float32
    )
    from_upper = passed_along(grad_edges[:HALF].astype(jnp.bfloat16), "seq", -1).astype(jnp.float32)
    grad_pair_local = (
        grad_edges[HALF : HALF + tok_count]
        + jnp.pad(from_lower, ((0, tok_count - HALF), (0, 0)))
        + jnp.pad(from_upper, ((tok_count - HALF, 0), (0, 0)))
    )
    grad_query_all = rotate_back(grad_queries.reshape(shape_three), cosine, sine)
    grad_key_all = rotate_back(grad_pair_local[:, :model_width].reshape(shape_three), cosine, sine)
    grad_mixed = jnp.concatenate(
        [
            grad_query_all.reshape(tok_count, model_width),
            grad_key_all.reshape(tok_count, model_width),
            grad_pair_local[:, model_width:],
        ],
        1,
    ).astype(jnp.bfloat16)
    grad_wqkv = inner_product(normed_low, grad_mixed)
    grad_normed_one = outer_product(grad_mixed, full_qkv)
    grad_input_norm, grad_first = norm_back(grad_normed_one, plain_one, spread_one, first_gain)
    grad_inputs = (grad_hidden + grad_input_norm).astype(jnp.bfloat16)
    partial_terms = (grad_wqkv, grad_wattn, grad_win, grad_wout, grad_first, grad_second)
    local_rows = (
        lax.psum_scatter(
            partial_terms[0].astype(jnp.bfloat16), "fsdp", scatter_dimension=0, tiled=True
        ).astype(jnp.float32),
        lax.psum_scatter(
            partial_terms[1].astype(jnp.bfloat16), "fsdp", scatter_dimension=0, tiled=True
        ).astype(jnp.float32),
        lax.psum_scatter(
            partial_terms[2].astype(jnp.bfloat16), "fsdp", scatter_dimension=0, tiled=True
        ).astype(jnp.float32),
        lax.psum_scatter(
            partial_terms[3].astype(jnp.bfloat16), "fsdp", scatter_dimension=0, tiled=True
        ).astype(jnp.float32),
        lax.psum_scatter(
            partial_terms[4].astype(jnp.bfloat16), "fsdp", scatter_dimension=0, tiled=True
        ).astype(jnp.float32),
        lax.psum_scatter(
            partial_terms[5].astype(jnp.bfloat16), "fsdp", scatter_dimension=0, tiled=True
        ).astype(jnp.float32),
    )
    shares = lax.psum(
        (local_rows[0], local_rows[1], local_rows[2], local_rows[3], local_rows[4], local_rows[5]),
        "seq",
    )
    return (
        output.astype(jnp.bfloat16)[None],
        grad_inputs[None],
        shares[0],
        shares[1],
        shares[2],
        shares[3],
        shares[4],
        shares[5],
    )


def solution(mesh):
    in_specs = (
        P("fsdp", "seq", None),
        P("fsdp", "seq", None),
        P("fsdp", None),
        P("fsdp", None),
        P("fsdp", None),
        P("fsdp", None),
        P("fsdp", None),
        P("fsdp"),
        P("fsdp"),
    )
    out_specs = (
        P("fsdp", "seq", None),
        P("fsdp", "seq", None),
        P("fsdp", None),
        P("fsdp", None),
        P("fsdp", None),
        P("fsdp", None),
        P("fsdp"),
        P("fsdp"),
    )
    return jax.shard_map(body, mesh=mesh, in_specs=in_specs, out_specs=out_specs, check_vma=False)
```

profile of v0, /device:TPU:0, one launch (start us, length us, event | category | flops | bytes accessed | tf_op | source)
XLA Modules:
  0.0 701.4 jit_solution(10764131211006831958)
XLA Ops:
  13.8 8.3 %all-reduce.8 = (bf16[768]{0:T(1024)(128)(2,1)S(1)}, bf16[768]{0:T(1024)(128)(2,1)S(1)}) all-reduce(bf16[768]{0:T(1024)(128)(2,1)S(1)} %dynamic-update-slice, bf16[768]{0:T(1024)(128)(2,1)S(1)} %dynamic-update-slice.1), channel_id=1, replica_groups=mesh['seq'=8,'fsdp'=4] {'fsdp'}, use_global_device_ids=true, to_apply=%add.2 | all-reduce | flops 1536 | bytes 6144
  31.4 3.6 copy.69
  34.9 8.1 %all-gather.5.cloned.1.call-done = bf16[768,2304]{1,0:T(8,128)(2,1)} async-done(((bf16[192,2304]{1,0:T(8,128)(2,1)}), bf16[768,2304]{1,0:T(8,128)(2,1)}) %all-gather.5.cloned.1.call-update) | async-done | bytes 3538960 | tf_op jit(solution)/shard_map/all_gather | solution.py:80
  43.1 6.0 fusion.58
  50.5 2.7 copy-done.7
  55.1 2.4 copy.70
  61.4 7.4 %fusion.70 = (f32[1024,768]{1,0:T(8,128)}, bf16[1024,768]{1,0:T(8,128)(2,1)}) fusion(f32[1024,2304]{1,0:T(8,128)} %copy-done.7, f32[1024,768]{1,0:T(8,128)} %copy.71, f32[1024,768]{1,0:T(8,128)} %copy.69), kind=kLoop, calls=%fused_computation.156 | loop fusion | flops 2359296 | bytes 17301504 | tf_op jit(solution)/shard_map/slice | solution.py:113
  68.8 2.6 copy.72
  73.1 3.3 collective-permute-start
  78.9 2.9 fusion.45
  81.8 3.3 collective-permute-done.1
  85.1 4.6 pad_maximum_fusion.2
  89.7 5.8 copy.73
  95.5 46.8 %while.26 = (s32[]{:T(128)}, bf16[2,512,768]{2,1,0:T(8,128)(2,1)}, f32[2,12,512]{2,1,0:T(8,128)S(1)}, s32[2]{0:T(128)S(1)}, bf16[1152,1536]{0,1:T(8,128)(2,1)}, ...) while((s32[]{:T(128)}, bf16[2,512,768]{2,1,0:T(8,128)(2,1)}, ...), condition=%wide.region_7.8_spmd.clone, body=%wide.region_4.7_spmd.clone.sunk | while | flops 1063315456 | bytes 59351292 | solution.py:155
  99.9 2.7 constant_dynamic-slice_fusion.5
  102.6 3.9 fusion.120
  106.5 4.8 fusion.121
  111.3 6.2 fusion.122
  123.2 2.6 constant_dynamic-slice_fusion.5
  125.8 3.9 fusion.120
  129.6 4.8 fusion.121
  134.4 6.2 fusion.122
  142.3 3.8 fusion.75
  148.2 10.7 %fusion.67 = f32[1024,2304]{1,0:T(8,128)} fusion(bf16[768,2304]{1,0:T(8,128)(2,1)} %all-gather.9.cloned.1.call-done, f32[1024,768]{0,1:T(8,128)} %copy-done.9, f32[768]{0:T(1024)S(1)} %copy-done.31, f32[1024]{0:T(1024)S(1)} %add_rsqrt_fusion, f32[1024]{0:T(1024)S(1)} %broadcast_multiply_fusion.6), kind=kOutput, calls=%fused_computation.154 | convolution fusion | flops 3627024384 | bytes 16133120 | tf_op jit(solution)/shard_map/dot_general | solution.py:160
  158.9 15.2 %add_convert_fusion = (bf16[1024,1152]{1,0:T(8,128)(2,1)S(1)}, f32[1024,1152]{1,0:T(8,128)S(1)}, f32[1024,1152]{1,0:T(8,128)S(1)}) fusion(f32[1024,2304]{1,0:T(8,128)} %fusion.67, bf16[1152,768]{1,0:T(8,128)(2,1)} %all-gather.11.cloned.1.call-done, bf16[1,1024,768]{2,1,0:T(8,128)(2,1)S(1)} %copy-done.24), kind=kOutput, calls=%fused_computation.44 | convolution fusion | flops 1898053632 | bytes 24576000 | tf_op jit(solution)/shard_map/dot_general | solution.py:42
  174.2 2.5 multiply_convert_fusion.1
  178.0 7.0 multiply_reduce_fusion.1
  187.7 2.5 convolution_convert_fusion.4
  190.2 4.9 convolution_convert_fusion.2
  195.2 9.3 %convolution_convert_fusion = bf16[768,2304]{1,0:T(8,128)(2,1)} fusion(bf16[1024,1152]{1,0:T(8,128)(2,1)} %copy-done.21, bf16[1024,1152]{1,0:T(8,128)(2,1)} %copy-done.41, f32[1024,768]{0,1:T(8,128)} %copy-done.9, f32[768]{0:T(1024)S(1)} %copy-done.31, f32[1024]{0:T(1024)S(1)} %add_rsqrt_fusion, f32[1024]{0:T(1024)S(1)} %broadcast_multiply_fusion.6), kind=kOutput, calls=%fused_computation.38 | convolution fusion | flops 3638231040 | bytes 11414528 | tf_op jit(solution)/shard_map/dot_general | solution.py:36
  205.8 4.5 convolution_convert_fusion.3
  210.3 3.4 broadcast_in_dim.95
  213.7 190.2 %while.27 = (s32[]{:T(128)}, f32[1152,1536]{0,1:T(8,128)}, f32[2,512,768]{1,0,2:T(2,128)}, s32[2]{0:T(128)S(1)}, bf16[1024,12,64]{0,2,1:T(8,128)(2,1)S(1)}, /*in...) while((s32[]{:T(128)}, f32[1152,1536]{0,1:T(8,128)}, ...), condition=%wide.region_14.15_spmd.clone, body=%wide.region_12.14_spmd.clone.sunk | while | flops 2556454912 | bytes 197640848 | solution.py:212
  220.9 2.7 fusion.132
  225.8 11.4 %multiply_reduce_fusion.7 = (f32[12,512]{1,0:T(8,128)}, f32[12,512,640]{2,1,0:T(8,128)}) fusion(f32[12,512,640]{2,1,0:T(8,128)S(1)} %fusion.133, f32[12,512]{1,0:T(8,128)} %dynamic-slice_bitcast_fusion.2, bf16[640,12,64]{0,2,1:T(8,128)(2,1)S(1)} %bitcast.172, bf16[1024,12,64]{0,2,1:T(8,128)(2,1)} %copy-done, s32[]{:T(128)S(6)} %select_n.83, ...), kind=kOutput, calls=%fused_computation.20.clone.1 | convolution fusion | flops 522971136 | bytes 33611780 | tf_op jit(solution)/shard_map/while/body/eval_jaxpr/qhd,khd->hqk/dot_general | solution.py:138
  237.2 6.9 multiply_convert_fusion.7
  244.1 7.1 %fusion.135 = f32[12,64,640]{2,1,0:T(8,128)S(1)} fusion(bf16[512,12,64]{0,2,1:T(8,128)(2,1)S(1)} %bitcast.176, f32[12,512,640]{2,1,0:T(8,128)} %get-tuple-element.511), kind=kOutput, calls=%fused_computation.22.clone.1 | convolution fusion | flops 507248640 | bytes 18481152 | tf_op jit(solution)/shard_map/while/body/eval_jaxpr/hqk,qhd->khd/dot_general | solution.py:198
  251.2 2.5 convolution_multiply_fusion.5
  253.8 2.9 convolution_multiply_fusion.4
  256.7 3.0 maximum_add_fusion.2
  261.3 28.6 %dynamic_update_slice.27 = f32[2,512,768]{1,0,2:T(2,128)} dynamic-update-slice(f32[2,512,768]{1,0,2:T(2,128)} %get-tuple-element.573, f32[1,512,768]{1,0,2:T(1,128)S(1)} %copy.105, s32[]{:T(128)S(6)} %copy.124, s32[]{:T(128)} %constant.81.clone.1..sunk.1, s32[]{:T(128)} %constant.81.clone.1..sunk.1) | dynamic-update-slice | bytes 3145732 | tf_op jit(solution)/shard_map/while/body/jit(dynamic_update_index_in_dim)/dynamic_update_slice | solution.py:155
  289.9 19.5 %dynamic_update_slice.26 = f32[1152,1536]{0,1:T(8,128)} dynamic-update-slice(f32[1152,1536]{0,1:T(8,128)} %get-tuple-element.572, f32[640,1536]{0,1:T(8,128)} %maximum_add_fusion.2, s32[]{:T(128)S(6)} %select_n.84, s32[]{:T(128)} %constant.81.clone.1..sunk.1) | dynamic-update-slice | bytes 7864324 | tf_op jit(solution)/shard_map/while/body/eval_jaxpr/dynamic_update_slice | solution.py:208
  316.3 2.6 fusion.132
  321.1 11.4 %multiply_reduce_fusion.7 = (f32[12,512]{1,0:T(8,128)}, f32[12,512,640]{2,1,0:T(8,128)}) fusion(f32[12,512,640]{2,1,0:T(8,128)S(1)} %fusion.133, f32[12,512]{1,0:T(8,128)} %dynamic-slice_bitcast_fusion.2, bf16[640,12,64]{0,2,1:T(8,128)(2,1)S(1)} %bitcast.172, bf16[1024,12,64]{0,2,1:T(8,128)(2,1)} %copy-done, s32[]{:T(128)S(6)} %select_n.83, ...), kind=kOutput, calls=%fused_computation.20.clone.1 | convolution fusion | flops 522971136 | bytes 33611780 | tf_op jit(solution)/shard_map/while/body/eval_jaxpr/qhd,khd->hqk/dot_general | solution.py:138
  332.5 6.9 multiply_convert_fusion.7
  339.3 7.0 %fusion.135 = f32[12,64,640]{2,1,0:T(8,128)S(1)} fusion(bf16[512,12,64]{0,2,1:T(8,128)(2,1)S(1)} %bitcast.176, f32[12,512,640]{2,1,0:T(8,128)} %get-tuple-element.511), kind=kOutput, calls=%fused_computation.22.clone.1 | convolution fusion | flops 507248640 | bytes 18481152 | tf_op jit(solution)/shard_map/while/body/eval_jaxpr/hqk,qhd->khd/dot_general | solution.py:198
  346.4 2.5 convolution_multiply_fusion.5
  348.9 2.9 convolution_multiply_fusion.4
  351.8 3.0 maximum_add_fusion.2
  356.4 28.5 %dynamic_update_slice.27 = f32[2,512,768]{1,0,2:T(2,128)} dynamic-update-slice(f32[2,512,768]{1,0,2:T(2,128)} %get-tuple-element.573, f32[1,512,768]{1,0,2:T(1,128)S(1)} %copy.105, s32[]{:T(128)S(6)} %copy.124, s32[]{:T(128)} %constant.81.clone.1..sunk.1, s32[]{:T(128)} %constant.81.clone.1..sunk.1) | dynamic-update-slice | bytes 3145732 | tf_op jit(solution)/shard_map/while/body/jit(dynamic_update_index_in_dim)/dynamic_update_slice | solution.py:155
  384.9 18.7 %dynamic_update_slice.26 = f32[1152,1536]{0,1:T(8,128)} dynamic-update-slice(f32[1152,1536]{0,1:T(8,128)} %get-tuple-element.572, f32[640,1536]{0,1:T(8,128)} %maximum_add_fusion.2, s32[]{:T(128)S(6)} %select_n.84, s32[]{:T(128)} %constant.81.clone.1..sunk.1) | dynamic-update-slice | bytes 7864324 | tf_op jit(solution)/shard_map/while/body/eval_jaxpr/dynamic_update_slice | solution.py:208
  403.9 3.5 convert.31
  408.4 5.4 collective-permute-start.2
  415.2 3.8 reshape.219
  419.7 9.6 %collective-permute-done.2 = bf16[64,1536]{0,1:T(8,128)(2,1)S(1)} collective-permute-done((bf16[64,1536]{0,1:T(8,128)(2,1)}, bf16[64,1536]{0,1:T(8,128)(2,1)S(1)}, u32[]{:S(2)}, u32[]{:S(2)}) %collective-permute-start.2) | collective-permute-done | bytes 196640 | tf_op jit(solution)/shard_map/ppermute | solution.py:32
  429.4 4.8 convert_add_fusion
  439.5 3.5 fusion.47
  443.0 7.6 %convolution_convert_fusion.1 = bf16[768,2304]{1,0:T(8,128)(2,1)} fusion(bf16[1024,768]{0,1:T(8,128)(2,1)S(1)} %slice.157, bf16[1024,768]{0,1:T(8,128)(2,1)} %get-tuple-element.361, bf16[1024,768]{0,1:T(8,128)(2,1)} %get-tuple-element.360, bf16[1,1024,768]{1,2,0:T(8,128)(2,1)S(1)} %copy-done.4, f32[768]{0:T(1024)S(1)} %copy-done.33, ...), kind=kOutput, calls=%fused_computation.39 | convolution fusion | flops 3643736064 | bytes 9841664 | tf_op jit(solution)/shard_map/dot_general | solution.py:36
  451.3 6.5 fusion.54
  457.8 2.8 copy.81
  460.6 8.5 %fusion.42 = (bf16[768]{0:T(1024)(128)(2,1)S(1)}, f32[1024]{0:T(1024)S(1)}, f32[1024]{0:T(1024)S(1)}, f32[1024,768]{0,1:T(8,128)S(1)}) fusion(bf16[1,1024,768]{1,2,0:T(8,128)(2,1)S(1)} %copy-done.4, f32[1024]{0:T(1024)S(1)} %copy-done.35, f32[1024]{0:T(1024)S(1)} %copy-done.30, f32[768]{0:T(1024)S(1)} %copy-done.33, ...), kind=kOutput, calls=%fused_computation.79 | convolution fusion | flops 3645109504 | bytes 12997120 | tf_op jit(solution)/shard_map/dot_general | solution.py:42
  471.7 6.2 all-reduce.7
  478.0 16.7 %reduce-scatter.5.cloned.1.call-done = bf16[192,2304]{1,0:T(8,128)(2,1)} async-done(((bf16[768,2304]{1,0:T(8,128)(2,1)}), bf16[192,2304]{1,0:T(8,128)(2,1)}) %reduce-scatter.5.cloned.1.call-update) | async-done | bytes 884752 | tf_op jit(solution)/shard_map/reduce_scatter | solution.py:238
  494.7 199.6 %all-reduce.10 = (f32[192,2304]{1,0:T(8,128)}, f32[192,768]{1,0:T(8,128)}, f32[192,2304]{1,0:T(8,128)}, f32[288,768]{1,0:T(8,128)}, f32[192]{0:T(256)}, /*index=5*/f32[192]{0:T(256)}) all-reduce(bf16[192,2304]{1,0:T(8,128)(2,1)} %reduce-scatter.5.cloned.1.call-done, ...), channel_id=1, replica_groups=mesh['seq'=8,'fsdp'=4] {'seq'}, use_global_device_ids=true, to_apply=%region_18.19 | all-reduce | flops 1253760 | bytes 7523328 | tf_op jit(solution)/shard_map/psum | solution.py:257
  (222 shorter events, 64.3 us)
Async XLA Ops:
  7.2 16.5 %copy-start.22 = (bf16[1,1024,768]{2,1,0:T(8,128)(2,1)S(1)}, bf16[1,1024,768]{2,1,0:T(8,128)(2,1)}, u32[]{:S(2)}) copy-start(bf16[1,1024,768]{2,1,0:T(8,128)(2,1)} %param.13) | copy-start | bytes 4718596
  7.2 35.9 %all-gather.5.cloned.1.call-start = ((), (), s32[]{:S(2)}) async-start(), calls=%async_computation.4 | async-start | bytes 4423680 | tf_op jit(solution)/shard_map/all_gather | solution.py:80
  7.9 134.4 %all-gather.7.cloned.1.call-start = ((), (), s32[]{:S(2)}) async-start(), calls=%async_computation.5 | async-start | bytes 1474560 | tf_op jit(solution)/shard_map/all_gather | solution.py:81
  8.7 139.5 %all-gather.9.cloned.1.call-start = ((), (), s32[]{:S(2)}) async-start(), calls=%async_computation.6 | async-start | bytes 4423680 | tf_op jit(solution)/shard_map/all_gather | solution.py:82
  9.4 149.5 %all-gather.11.cloned.1.call-start = ((), (), s32[]{:S(2)}) async-start(), calls=%async_computation.7 | async-start | bytes 2211840 | tf_op jit(solution)/shard_map/all_gather | solution.py:83
  10.0 468.1 %reduce-scatter.7.cloned.1.call-start = ((), (), s32[]{:S(2)}) async-start(), calls=%async_computation.9 | async-start | bytes 1474560 | tf_op jit(solution)/shard_map/reduce_scatter | solution.py:241
  22.1 20.9 %copy-start.32 = (f32[768]{0:T(1024)}, f32[768]{0:T(1024)S(1)}, u32[]{:S(2)}) copy-start(f32[768]{0:T(1024)S(1)} %convert_element_type.113) | copy-start | bytes 9220
  24.4 18.7 %copy-start.3 = (bf16[1,1024,768]{1,2,0:T(8,128)(2,1)}, bf16[1,1024,768]{1,2,0:T(8,128)(2,1)S(1)}, u32[]{:S(2)}) copy-start(bf16[1,1024,768]{1,2,0:T(8,128)(2,1)S(1)} %copy.68) | copy-start | bytes 4718596
  24.4 2.0 copy-start.23
  24.7 18.4 %copy-start.29 = (f32[1024]{0:T(1024)}, f32[1024]{0:T(1024)S(1)}, u32[]{:S(2)}) copy-start(f32[1024]{0:T(1024)S(1)} %broadcast_multiply_fusion.7) | copy-start | bytes 12292
  26.4 16.7 %copy-start.34 = (f32[1024]{0:T(1024)}, f32[1024]{0:T(1024)S(1)}, u32[]{:S(2)}) copy-start(f32[1024]{0:T(1024)S(1)} %add_rsqrt_fusion.1) | copy-start | bytes 12292
  29.3 48.9 %copy-start.16 = (f32[1024,64]{0,1:T(8,128)}, f32[1024,64]{0,1:T(8,128)S(1)}, u32[]{:S(2)}) copy-start(f32[1024,64]{0,1:T(8,128)S(1)} %get-tuple-element.373) | copy-start | bytes 786436
  49.1 4.2 copy-start.7
  71.5 6.7 copy-start.2
  73.1 8.8 %collective-permute-start = (bf16[64,1536]{1,0:T(8,128)(2,1)S(1)}, bf16[64,1536]{1,0:T(8,128)(2,1)S(1)}, u32[]{:S(2)}, u32[]{:S(2)}) collective-permute-start(bf16[64,1536]{1,0:T(8,128)(2,1)S(1)} %get-tuple-element.356), channel_id=1, source_target_pairs={{0,4},{4,8},{8,12},{12,16},{16,20},{20,24},{24,28},{1,5},{5,9},{9,... | collective-permute-start | bytes 589832 | tf_op jit(solution)/shard_map/ppermute | solution.py:23
  76.4 8.7 %collective-permute-start.1 = (bf16[64,1536]{1,0:T(8,128)(2,1)S(1)}, bf16[64,1536]{1,0:T(8,128)(2,1)S(1)}, u32[]{:S(2)}, u32[]{:S(2)}) collective-permute-start(bf16[64,1536]{1,0:T(8,128)(2,1)S(1)} %get-tuple-element.357), channel_id=1, source_target_pairs={{4,0},{8,4},{12,8},{16,12},{20,16},{24,20},{28,24},{5,1},{9,5},{13... | collective-permute-start | bytes 589832 | tf_op jit(solution)/shard_map/ppermute | solution.py:24
  78.9 6.2 copy-start.5
  78.9 6.2 copy-start.6
  146.1 1.6 copy-start.9
  146.1 2.1 copy-start.31
  148.2 10.8 %copy-start.24 = (bf16[1,1024,768]{2,1,0:T(8,128)(2,1)S(1)}, bf16[1,1024,768]{2,1,0:T(8,128)(2,1)}, u32[]{:S(2)}) copy-start(bf16[1,1024,768]{2,1,0:T(8,128)(2,1)} %param.14) | copy-start | bytes 4718596
  158.9 15.2 %copy-start.14 = (f32[1024,2304]{1,0:T(8,128)S(1)}, f32[1024,2304]{1,0:T(8,128)}, u32[]{:S(2)}) copy-start(f32[1024,2304]{1,0:T(8,128)} %fusion.67) | copy-start | bytes 28311556
  174.2 2.6 copy-start.41
  174.2 3.8 copy-start.10
  176.7 8.2 %copy-start.21 = (bf16[1024,1152]{1,0:T(8,128)(2,1)}, bf16[1024,1152]{1,0:T(8,128)(2,1)S(1)}, u32[]{:S(2)}) copy-start(bf16[1024,1152]{1,0:T(8,128)(2,1)S(1)} %get-tuple-element.344) | copy-start | bytes 7077892
  178.0 7.0 copy-start.15
  185.0 2.7 copy-start.37
  186.0 1.7 copy-start.12
  190.2 287.9 %reduce-scatter.11.cloned.1.call-start = ((), (), s32[]{:S(2)}) async-start(), calls=%async_computation.11 | async-start | bytes 2211840 | tf_op jit(solution)/shard_map/reduce_scatter | solution.py:247
  195.2 282.9 %reduce-scatter.9.cloned.1.call-start = ((), (), s32[]{:S(2)}) async-start(), calls=%async_computation.10 | async-start | bytes 4423680 | tf_op jit(solution)/shard_map/reduce_scatter | solution.py:244
  204.5 1.3 copy-start.38
  204.6 290.2 %reduce-scatter.5.cloned.1.call-start = ((), (), s32[]{:S(2)}) async-start(), calls=%async_computation.8 | async-start | bytes 4423680 | tf_op jit(solution)/shard_map/reduce_scatter | solution.py:238
  214.0 4.1 copy-start.25
  214.1 4.1 copy-start.27
  214.1 4.1 copy-start.39
  214.1 6.8 copy-start
  251.2 5.5 slice-start
  253.7 3.0 slice-start.1
  289.9 19.5 %copy-start.1 = (bf16[1024,12,64]{0,2,1:T(8,128)(2,1)S(1)}, bf16[1024,12,64]{0,2,1:T(8,128)(2,1)}, u32[]{:S(2)}) copy-start(bf16[1024,12,64]{0,2,1:T(8,128)(2,1)} %copy-done) | copy-start | bytes 4718596 | tf_op jit(solution)/shard_map/while
  289.9 19.5 %copy-start.26 = (f32[2,12,512]{2,1,0:T(8,128)S(1)}, f32[2,12,512]{2,1,0:T(8,128)}, u32[]{:S(2)}) copy-start(f32[2,12,512]{2,1,0:T(8,128)} %copy-done.25) | copy-start | bytes 147460 | tf_op jit(solution)/shard_map/while
  289.9 19.5 %copy-start.28 = (s32[1024]{0:T(1024)S(1)}, s32[1024]{0:T(1024)}, u32[]{:S(2)}) copy-start(s32[1024]{0:T(1024)} %copy-done.27) | copy-start | bytes 12292 | tf_op jit(solution)/shard_map/while
  289.9 19.5 %copy-start.40 = (s32[2]{0:T(128)S(1)}, s32[2]{0:T(128)}, u32[]{:S(2)}) copy-start(s32[2]{0:T(128)} %copy-done.39) | copy-start | bytes 28 | tf_op jit(solution)/shard_map/while
  309.4 4.1 copy-start.25
  309.5 4.1 copy-start.27
  309.5 4.1 copy-start.39
  309.5 6.8 copy-start
  346.4 5.4 slice-start
  348.9 2.9 slice-start.1
  384.9 18.7 %copy-start.1 = (bf16[1024,12,64]{0,2,1:T(8,128)(2,1)S(1)}, bf16[1024,12,64]{0,2,1:T(8,128)(2,1)}, u32[]{:S(2)}) copy-start(bf16[1024,12,64]{0,2,1:T(8,128)(2,1)} %copy-done) | copy-start | bytes 4718596 | tf_op jit(solution)/shard_map/while
  384.9 18.7 %copy-start.26 = (f32[2,12,512]{2,1,0:T(8,128)S(1)}, f32[2,12,512]{2,1,0:T(8,128)}, u32[]{:S(2)}) copy-start(f32[2,12,512]{2,1,0:T(8,128)} %copy-done.25) | copy-start | bytes 147460 | tf_op jit(solution)/shard_map/while
  384.9 18.7 %copy-start.28 = (s32[1024]{0:T(1024)S(1)}, s32[1024]{0:T(1024)}, u32[]{:S(2)}) copy-start(s32[1024]{0:T(1024)} %copy-done.27) | copy-start | bytes 12292 | tf_op jit(solution)/shard_map/while
  384.9 18.7 %copy-start.40 = (s32[2]{0:T(128)S(1)}, s32[2]{0:T(128)}, u32[]{:S(2)}) copy-start(s32[2]{0:T(128)} %copy-done.39) | copy-start | bytes 28 | tf_op jit(solution)/shard_map/while
  403.8 11.3 %copy-start.8 = (f32[2,512,768]{1,0,2:T(2,128)S(1)}, f32[2,512,768]{1,0,2:T(2,128)}, u32[]{:S(2)}) copy-start(f32[2,512,768]{1,0,2:T(2,128)} %get-tuple-element.116) | copy-start | bytes 9437188
  408.4 20.9 %collective-permute-start.2 = (bf16[64,1536]{0,1:T(8,128)(2,1)}, bf16[64,1536]{0,1:T(8,128)(2,1)S(1)}, u32[]{:S(2)}, u32[]{:S(2)}) collective-permute-start(bf16[64,1536]{0,1:T(8,128)(2,1)} %get-tuple-element.348), channel_id=1, source_target_pairs={{0,4},{4,8},{8,12},{12,16},{16,20},{20,24},{24,28},{1,5},{5,9},{9,... | collective-permute-start | bytes 589832 | tf_op jit(solution)/shard_map/ppermute | solution.py:32
  413.9 15.5 %collective-permute-start.3 = (bf16[64,1536]{0,1:T(8,128)(2,1)}, bf16[64,1536]{0,1:T(8,128)(2,1)}, u32[]{:S(2)}, u32[]{:S(2)}) collective-permute-start(bf16[64,1536]{0,1:T(8,128)(2,1)} %get-tuple-element.349), channel_id=1, source_target_pairs={{4,0},{8,4},{12,8},{16,12},{20,16},{24,20},{28,24},{5,1},{9,5},{13... | collective-permute-start | bytes 589832 | tf_op jit(solution)/shard_map/ppermute | solution.py:32
  434.4 1.9 copy-start.11
  434.4 1.9 copy-start.20
  438.5 1.0 copy-start.17
  439.5 3.5 copy-start.4
  439.5 3.5 copy-start.30
  439.5 3.5 copy-start.33
  439.5 3.5 copy-start.35
  460.6 8.5 %copy-start.13 = (f32[1024,768]{0,1:T(8,128)S(1)}, f32[1024,768]{0,1:T(8,128)}, u32[]{:S(2)}) copy-start(f32[1024,768]{0,1:T(8,128)} %copy-done.12) | copy-start | bytes 9437188
  470.2 1.6 copy-start.36
  (2 other events, 1.9 us)
Sparse Core Ops, SparseCore 0:
  9.6 33.4 all-gather.4
  44.6 17.4 all-gather.6
  63.7 30.7 all-gather.8
  95.9 20.7 all-gather.10
  190.3 26.9 reduce-scatter.6
  220.5 29.3 reduce-scatter.10
  252.4 40.4 reduce-scatter.8
  450.7 43.9 reduce-scatter.4
where the time goes:
time: 715 us; the launch traced here: 701 us
  blocking collectives  214 us (30%)
  local copies, waits for them, and re-layouts  174 us (24%)
  matrix products  159 us (22%)
  other arithmetic  71.8 us (10%)
  waiting for transfers between devices  40.4 us (6%)
  between operations  16.3 us (2%)
  loops' own time  14.3 us (2%)
  starting transfers between devices  11.9 us (2%)
    psum x1, blocking collectives, body(): lax.psum((local_rows[0], local_rows[1], local_rows[2], local_rows[3], loc...  200 us
    dynamic_update_slice x8, local copies, waits for them, and re-layouts, body(): context_blocks, log_totals = lax.map(forward_block, beginnings)  62.7 us
    dynamic_update_slice x2, local copies, waits for them, and re-layouts, backward_block(): lax.dynamic_update_slice_in_dim(carried, current + grad_pair, begin, 0)  38.2 us
    dot_general x4, matrix products, outer_product(): lax.dot_general(left, right, (((1,), (1,)), ((), ())), preferred_element_...  35.1 us
    dot_general x4, matrix products, block_inputs(): jnp.einsum('qhd,khd->hqk', query_block, key_block, preferred_element_type...  30.5 us
    unnamed x79, local copies, waits for them, and re-layouts  29.3 us
    dot_general x4, matrix products, inner_product(): lax.dot_general(left, right, (((0,), (0,)), ((), ())), preferred_element_...  24.3 us
    reduce_scatter x1, waiting for transfers between devices, body(): lax.psum_scatter(partial_terms[0].astype(jnp.bfloat16), 'fsdp', scatter_d...  16.7 us
  transfers between devices with their start and end apart: 12, of which 4 were waited for; matrix products, arithmetic and copies ran while one was open for 52% of the time, Pallas kernels for 0%

commit v1 on v0

v1 whole, which is shorter than its diff:
```python
import math

import jax
import jax.numpy as jnp
from jax import lax
from jax.experimental import pallas as pl
from jax.experimental.pallas import tpu as pltpu
from jax.sharding import PartitionSpec as P

HEADS = 12
HALF = 64
BLOCK = 128
SPAN = BLOCK + 2 * HALF
LANES = 128
VMEM_LIMIT = 48 * 1024 * 1024


EPSILON = 1e-05
THETA = 10000.0


def inner_product(left, right):
    return lax.dot_general(
        left, right, (((0,), (0,)), ((), ())), preferred_element_type=jnp.float32
    )


def outer_product(left, right):
    return lax.dot_general(
        left, right, (((1,), (1,)), ((), ())), preferred_element_type=jnp.float32
    )


def norm_parts(values, gain):
    average = jnp.mean(values, -1, keepdims=True)
    centred = values - average
    spread = lax.rsqrt(jnp.mean(centred * centred, -1, keepdims=True) + EPSILON)
    plain = centred * spread
    return (plain, spread, plain * gain)


def norm_back(grad_normed, plain, spread, gain):
    grad_plain = grad_normed * gain
    grad_values = spread * (
        grad_plain
        - jnp.mean(grad_plain, -1, keepdims=True)
        - plain * jnp.mean(grad_plain * plain, -1, keepdims=True)
    )
    return (grad_values, jnp.sum(grad_normed * plain, 0))


def lane_index(rows):
    return lax.broadcasted_iota(jnp.int32, (rows, LANES), 1)


def turned(values, direction):
    first_half = lax.rem(lane_index(values.shape[0]), 64) < 32
    ahead = pltpu.roll(values, LANES - 32, 1)
    behind = pltpu.roll(values, 32, 1)
    return jnp.where(first_half, -direction * ahead, direction * behind)


def pair_rows(values):
    low = lane_index(values.shape[0]) < 64
    zero = jnp.zeros_like(values)
    return jnp.concatenate([jnp.where(low, values, zero), jnp.where(low, zero, values)], 0)


def pair_lanes(stacked):
    rows = stacked.shape[0] // 2
    return jnp.where(lane_index(rows) < 64, stacked[:rows], stacked[rows:])


def attend_kernel(
    bounds, mq, mk, mv, cosine, sine, query, key, value, context, probs, bias_ref
):
    tokens = context.shape[0]
    blocks = tokens // BLOCK
    base = bounds[3]
    group_length = bounds[4]

    @pl.when(pl.program_id(0) == 0)
    def _():
        def ident(place):
            found = jnp.zeros_like(place)
            for index in range(3):
                found = found + (place >= bounds[index]).astype(jnp.int32)
            return jnp.where(place >= group_length, -2, found)

        rows = lax.broadcasted_iota(jnp.int32, (BLOCK, SPAN), 0)
        columns = lax.broadcasted_iota(jnp.int32, (BLOCK, SPAN), 1)
        near = jnp.abs(columns - HALF - rows) <= HALF
        for block in range(blocks):
            begin = base + block * BLOCK
            same = ident(begin + rows) == ident(begin - HALF + columns)
            bias_ref[block] = jnp.where(near & same, 0.0, -1e30)

    table_cos = cosine[...]
    table_sin = sine[...]

    def rope(values):
        return values * table_cos + turned(values, 1.0) * table_sin

    query[...] = rope(mq[...]).astype(jnp.bfloat16)
    key[...] = rope(mk[...]).astype(jnp.bfloat16)
    value[...] = mv[...].astype(jnp.bfloat16)
    for block in range(blocks):
        begin = block * BLOCK
        stacked = pair_rows(query[begin + HALF : begin + HALF + BLOCK] * jnp.bfloat16(0.125))
        keys = key[begin : begin + SPAN]
        scores = lax.dot_general(
            stacked, keys, (((1,), (1,)), ((), ())), preferred_element_type=jnp.float32
        )
        bias = bias_ref[block]
        scores = scores + jnp.concatenate([bias, bias], 0)
        highest = jnp.max(scores, 1, keepdims=True)
        weights = jnp.exp(scores - highest)
        totals = jnp.sum(weights, 1, keepdims=True)
        shares = (weights * (1.0 / totals)).astype(jnp.bfloat16)
        probs[0, block] = shares
        mixed = jnp.dot(shares, value[begin : begin + SPAN], preferred_element_type=jnp.float32)
        context[begin : begin + BLOCK] = pair_lanes(mixed).astype(jnp.bfloat16)


def attend_back_kernel(
    query, key, value, probs, grad_context, cosine, sine, grad_mixed, grad_edges, key_sum, value_sum
):
    tokens = grad_context.shape[0]
    width = grad_mixed.shape[1] // 3
    pair = pl.program_id(0)
    key_sum[...] = jnp.zeros_like(key_sum)
    value_sum[...] = jnp.zeros_like(value_sum)

    def columns(part):
        return pl.ds(pl.multiple_of(part * width + pair * LANES, LANES), LANES)

    def unrope(grads, rows):
        return grads * cosine[rows] - turned(grads, 1.0) * sine[rows]

    for block in range(tokens // BLOCK):
        begin = block * BLOCK
        own = slice(begin + HALF, begin + HALF + BLOCK)
        window = slice(begin, begin + SPAN)
        stacked = pair_rows(query[own] * jnp.bfloat16(0.125))
        grads = pair_rows(grad_context[begin : begin + BLOCK])
        low_probs = probs[0, block]
        shares = low_probs.astype(jnp.float32)
        grad_probs = lax.dot_general(
            grads, value[window], (((1,), (1,)), ((), ())), preferred_element_type=jnp.float32
        )
        delta = jnp.sum(shares * grad_probs, 1, keepdims=True)
        grad_scores = (shares * (grad_probs - delta)).astype(jnp.bfloat16)
        grad_query = pair_lanes(
            jnp.dot(grad_scores, key[window], preferred_element_type=jnp.float32)
        )
        grad_mixed[begin : begin + BLOCK, columns(0)] = unrope(grad_query * 0.125, own).astype(
            jnp.bfloat16
        )
        key_sum[window] += lax.dot_general(
            grad_scores, stacked, (((0,), (0,)), ((), ())), preferred_element_type=jnp.float32
        )
        value_sum[window] += lax.dot_general(
            low_probs, grads, (((0,), (0,)), ((), ())), preferred_element_type=jnp.float32
        )
    everything = slice(0, tokens + 2 * HALF)
    grad_key = unrope(key_sum[...], everything).astype(jnp.bfloat16)
    grad_value = value_sum[...].astype(jnp.bfloat16)
    for part, grads in ((1, grad_key), (2, grad_value)):
        grad_mixed[:, columns(part)] = grads[HALF : HALF + tokens]
        grad_edges[:HALF, columns(part - 1)] = grads[:HALF]
        grad_edges[HALF:, columns(part - 1)] = grads[HALF + tokens :]


def attend(bounds, mixed, cosine, sine, tokens):
    rows, width = mixed.shape[0], mixed.shape[1] // 3
    pairs = width // LANES
    blocks = tokens // BLOCK

    def part(index):
        return pl.BlockSpec((rows, LANES), lambda p, *_: (0, p + index * pairs))

    table = pl.BlockSpec((rows, LANES), lambda p, *_: (0, 0))
    low = lambda count: jax.ShapeDtypeStruct((count, width), jnp.bfloat16)
    return pl.pallas_call(
        attend_kernel,
        grid_spec=pltpu.PrefetchScalarGridSpec(
            num_scalar_prefetch=1,
            grid=(pairs,),
            in_specs=[part(0), part(1), part(2), table, table],
            out_specs=[
                part(0),
                part(0),
                part(0),
                pl.BlockSpec((tokens, LANES), lambda p, *_: (0, p)),
                pl.BlockSpec((1, blocks, 2 * BLOCK, SPAN), lambda p, *_: (p, 0, 0, 0)),
            ],
            scratch_shapes=[pltpu.VMEM((blocks, BLOCK, SPAN), jnp.float32)],
        ),
        out_shape=[
            low(rows),
            low(rows),
            low(rows),
            low(tokens),
            jax.ShapeDtypeStruct((pairs, blocks, 2 * BLOCK, SPAN), jnp.bfloat16),
        ],
        compiler_params=pltpu.CompilerParams(vmem_limit_bytes=VMEM_LIMIT),
        name="attend",
    )(bounds, mixed, mixed, mixed, cosine, sine)


def attend_back(query, key, value, probs, grad_context, cosine, sine):
    tokens, width = grad_context.shape
    rows = query.shape[0]
    pairs = width // LANES
    blocks = tokens // BLOCK
    lanes = pl.BlockSpec((rows, LANES), lambda p: (0, p))
    table = pl.BlockSpec((rows, LANES), lambda p: (0, 0))
    return pl.pallas_call(
        attend_back_kernel,
        grid=(pairs,),
        in_specs=[
            lanes,
            lanes,
            lanes,
            pl.BlockSpec((1, blocks, 2 * BLOCK, SPAN), lambda p: (p, 0, 0, 0)),
            pl.BlockSpec((tokens, LANES), lambda p: (0, p)),
            table,
            table,
        ],
        out_specs=[
            pl.BlockSpec((tokens, 3 * width), lambda p: (0, 0)),
            pl.BlockSpec((2 * HALF, 2 * width), lambda p: (0, 0)),
        ],
        out_shape=[
            jax.ShapeDtypeStruct((tokens, 3 * width), jnp.bfloat16),
            jax.ShapeDtypeStruct((2 * HALF, 2 * width), jnp.bfloat16),
        ],
        scratch_shapes=[
            pltpu.VMEM((rows, LANES), jnp.float32),
            pltpu.VMEM((rows, LANES), jnp.float32),
        ],
        compiler_params=pltpu.CompilerParams(vmem_limit_bytes=VMEM_LIMIT),
        name="attend_back",
    )(query, key, value, probs, grad_context, cosine, sine)


def passed_along(value, axis, steps):
    count = lax.axis_size(axis)
    first, last = (max(0, -steps), min(count, count - steps))
    return lax.ppermute(value, axis, [(source, source + steps) for source in range(first, last)])


def summed_rows(partial):
    rows = lax.psum_scatter(
        partial.astype(jnp.bfloat16), "fsdp", scatter_dimension=0, tiled=True
    )
    count = rows.shape[0]
    padding = -count % (8 * lax.axis_size("seq"))
    if padding:
        rows = jnp.pad(rows, ((0, padding), (0, 0)))
    share = lax.psum_scatter(rows, "seq", scatter_dimension=0, tiled=True)
    return lax.all_gather(share, "seq", axis=0, tiled=True)[:count].astype(jnp.float32)


def body(tokens, cotangent, starts, w_qkv, w_attn, w_in, w_out, gain_one, gain_two):
    tok_count, model_width = tokens.shape[1:]
    head_size = model_width // HEADS
    before = passed_along(tokens[0, tok_count - HALF :], "seq", 1)
    after = passed_along(tokens[0, :HALF], "seq", -1)
    gains = lax.all_gather(jnp.stack([gain_one, gain_two]), "fsdp", axis=1, tiled=True)
    full_qkv, full_attn, full_in, full_out = (
        lax.all_gather(w_qkv, "fsdp", axis=0, tiled=True),
        lax.all_gather(w_attn, "fsdp", axis=0, tiled=True),
        lax.all_gather(w_in, "fsdp", axis=0, tiled=True),
        lax.all_gather(w_out, "fsdp", axis=0, tiled=True),
    )
    first_gain = gains[0].astype(jnp.float32)
    second_gain = gains[1].astype(jnp.float32)
    extended = jnp.concatenate([before, tokens[0], after], 0).astype(jnp.float32)
    inputs = tokens[0].astype(jnp.float32)
    ff_width = full_out.shape[0]
    seq_index = lax.axis_index("seq")
    group_length = tok_count * lax.axis_size("seq")
    seq_starts = starts[0]
    places = seq_index * tok_count - HALF + jnp.arange(tok_count + 2 * HALF, dtype=jnp.int32)
    earlier = seq_starts[None, :] <= places[:, None]
    first_token = jnp.max(jnp.where(earlier, seq_starts[None, :], 0), 1)
    position = (places - first_token).astype(jnp.float32)
    freqs = THETA ** (-jnp.arange(head_size // 2, dtype=jnp.float32) * 2.0 / head_size)
    angles = position[:, None] * freqs[None, :]
    cosine = jnp.tile(jnp.cos(angles), (1, LANES // (head_size // 2)))
    sine = jnp.tile(jnp.sin(angles), (1, LANES // (head_size // 2)))
    bounds = jnp.concatenate(
        [
            seq_starts,
            jnp.stack([seq_index * tok_count, jnp.int32(group_length)]).astype(jnp.int32),
        ]
    )
    normed_ext = norm_parts(extended, first_gain)[2].astype(jnp.bfloat16)
    mixed = jnp.dot(normed_ext, full_qkv, preferred_element_type=jnp.float32)
    query, key, value, context, probs = attend(bounds, mixed, cosine, sine, tok_count)
    hidden = inputs + jnp.dot(context, full_attn, preferred_element_type=jnp.float32)
    plain_two, spread_two, normed_two = norm_parts(hidden, second_gain)
    normed_two_low = normed_two.astype(jnp.bfloat16)
    both = jnp.dot(normed_two_low, full_in, preferred_element_type=jnp.float32)
    gate = both[:, :ff_width]
    upper = both[:, ff_width:]
    active, gelu_back = jax.vjp(lambda entry: jax.nn.gelu(entry, approximate=False), gate)
    act_low = (active * upper).astype(jnp.bfloat16)
    output = hidden + jnp.dot(act_low, full_out, preferred_element_type=jnp.float32)
    grad_result = cotangent[0]
    grad_wout = inner_product(act_low, grad_result)
    grad_act = outer_product(grad_result, full_out)
    grad_gate = gelu_back(grad_act * upper)[0]
    grad_both = jnp.concatenate([grad_gate, grad_act * active], 1).astype(jnp.bfloat16)
    grad_win = inner_product(normed_two_low, grad_both)
    grad_normed_two = outer_product(grad_both, full_in)
    grad_hidden_norm, grad_second = norm_back(grad_normed_two, plain_two, spread_two, second_gain)
    grad_hidden = grad_result.astype(jnp.float32) + grad_hidden_norm
    grad_hidden_low = grad_hidden.astype(jnp.bfloat16)
    grad_wattn = inner_product(context, grad_hidden_low)
    grad_context = outer_product(grad_hidden_low, full_attn).astype(jnp.bfloat16)

    grad_mixed, grad_edges = attend_back(query, key, value, probs, grad_context, cosine, sine)
    from_lower = passed_along(grad_edges[HALF:], "seq", 1)
    from_upper = passed_along(grad_edges[:HALF], "seq", -1)
    grad_mixed = grad_mixed.at[:HALF, model_width:].add(from_lower)
    grad_mixed = grad_mixed.at[tok_count - HALF :, model_width:].add(from_upper)
    normed_low = normed_ext[HALF : HALF + tok_count]
    plain_one, spread_one, _ = norm_parts(inputs, first_gain)
    grad_wqkv = inner_product(normed_low, grad_mixed)
    grad_normed_one = outer_product(grad_mixed, full_qkv)
    grad_input_norm, grad_first = norm_back(grad_normed_one, plain_one, spread_one, first_gain)
    grad_inputs = (grad_hidden + grad_input_norm).astype(jnp.bfloat16)
    sums = lax.psum(jnp.stack([grad_first, grad_second]), ("seq", "fsdp"))
    rows = gain_one.shape[0]
    own_gains = lax.dynamic_slice_in_dim(sums, lax.axis_index("fsdp") * rows, rows, 1)
    return (
        output.astype(jnp.bfloat16)[None],
        grad_inputs[None],
        summed_rows(grad_wqkv),
        summed_rows(grad_wattn),
        summed_rows(grad_win),
        summed_rows(grad_wout),
        own_gains[0],
        own_gains[1],
    )


def solution(mesh):
    in_specs = (
        P("fsdp", "seq", None),
        P("fsdp", "seq", None),
        P("fsdp", None),
        P("fsdp", None),
        P("fsdp", None),
        P("fsdp", None),
        P("fsdp", None),
        P("fsdp"),
        P("fsdp"),
    )
    out_specs = (
        P("fsdp", "seq", None),
        P("fsdp", "seq", None),
        P("fsdp", None),
        P("fsdp", None),
        P("fsdp", None),
        P("fsdp", None),
        P("fsdp"),
        P("fsdp"),
    )
    return jax.shard_map(body, mesh=mesh, in_specs=in_specs, out_specs=out_specs, check_vma=False)
```

time: 715 us -> 595 us (0.83)
  local copies, waits for them, and re-layouts: 174 us -> 26.1 us
  waiting for transfers between devices: 40.4 us -> 187 us
  matrix products: 159 us -> 93.3 us
  Pallas kernels: 0 us -> 54.8 us
  other arithmetic: 71.8 us -> 25 us
  blocking collectives: 214 us -> 174 us
  loops' own time: 14.3 us -> 0 us
    psum x1, blocking collectives: 200 us -> 39.5 us  [body(): sums = lax.psum(jnp.stack([grad_first, grad_second]), ('seq', 'fsdp'))]
    reduce_scatter x4 -> x8, waiting for transfers between devices: 16.7 us -> 160 us  [the longest x4 107 us: summed_rows(): share = lax.psum_scatter(rows, 'seq', scatter_dimension=0, tiled=True)]
    all_gather x0 -> x5, blocking collectives: none -> 134 us  [the longest x4 129 us: summed_rows(): lax.all_gather(share, 'seq', axis=0, tiled=True)[:count].astype(jnp.float32)]
    dynamic_update_slice x10 -> x0, local copies, waits for them, and re-layouts: 101 us -> none  [the longest x8 62.7 us: body(): context_blocks, log_totals = lax.map(forward_block, beginnings)]
    dot_general x15 -> x1, matrix products: 78.4 us -> 10.9 us  [body(): mixed = jnp.dot(normed_ext, full_qkv, preferred_element_type=jnp.float32)]
    pallas_call x0 -> x2, Pallas kernels: none -> 54.8 us  [the longest x1 28.9 us: attend(): pl.pallas_call(attend_kernel, grid_spec=pltpu.PrefetchScalarGridSpec(num_...]
    slice x12 -> x2, local copies, waits for them, and re-layouts: 20.6 us -> 0.67 us  [the longest x1 0.64 us: body(): own_gains[1]]
    unnamed x79 -> x37, local copies, waits for them, and re-layouts: 29.3 us -> 13.4 us
  transfers between devices with their start and end apart: 12 -> 16, of which waited for: 4 -> 10; matrix products, arithmetic and copies ran while one was open for 52% -> 19% of each run, Pallas kernels for 0% -> 9%
where the time goes in v1:
time: 595 us; the launch traced here: 587 us
  waiting for transfers between devices  187 us (31%)
  blocking collectives  174 us (29%)
  matrix products  93.3 us (16%)
  Pallas kernels  54.8 us (9%)
  local copies, waits for them, and re-layouts  26.1 us (4%)
  other arithmetic  25 us (4%)
  between operations  15.1 us (3%)
  starting transfers between devices  11.8 us (2%)
    all_gather x4, blocking collectives, summed_rows(): lax.all_gather(share, 'seq', axis=0, tiled=True)[:count].astype(jnp.float32)  129 us
    reduce_scatter x4, waiting for transfers between devices, summed_rows(): share = lax.psum_scatter(rows, 'seq', scatter_dimension=0, tiled=True)  107 us
    reduce_scatter x4, waiting for transfers between devices, summed_rows(): lax.psum_scatter(partial.astype(jnp.bfloat16), 'fsdp', scatter_dimension=...  53 us
    psum x1, blocking collectives, body(): sums = lax.psum(jnp.stack([grad_first, grad_second]), ('seq', 'fsdp'))  39.5 us
    dot_general x4, matrix products, outer_product(): lax.dot_general(left, right, (((1,), (1,)), ((), ())), preferred_element_...  36.8 us
    pallas_call x1, Pallas kernels, attend(): pl.pallas_call(attend_kernel, grid_spec=pltpu.PrefetchScalarGridSpec(num_...  28.9 us
    pallas_call x1, Pallas kernels, attend_back(): pl.pallas_call(attend_back_kernel, grid=(pairs,), in_specs=[lanes, lanes,...  25.8 us
    dot_general x4, matrix products, inner_product(): lax.dot_general(left, right, (((0,), (0,)), ((), ())), preferred_element_...  25.8 us
  transfers between devices with their start and end apart: 16, of which 10 were waited for; matrix products, arithmetic and copies ran while one was open for 19% of the time, Pallas kernels for 9%

profile of v1, /device:TPU:0, one launch (start us, length us, event | category | flops | bytes accessed | tf_op | source)
XLA Modules:
  0.0 586.7 jit_solution(15329843428796600934)
XLA Ops:
  7.2 0.7 all-gather.6.cloned.1.call-update
  8.0 0.7 all-gather.8.cloned.1.call-update
  8.7 0.7 all-gather.10.cloned.1.call-update
  9.5 1.7 copy.59
  11.2 0.9 slice_bitcast_fusion
  12.1 5.5 collective-permute-start
  17.6 1.3 collective-permute-start.1
  19.1 5.1 all-gather
  25.6 2.6 copy.66
  28.3 4.0 concatenate.15
  32.2 1.9 convert_reduce_fusion.1
  34.2 2.0 fusion.14
  36.2 1.8 fusion.16
  37.9 5.2 all-gather.6.cloned.1.call-done
  43.1 10.9 %fusion.44.mq.mk.mv = f32[1152,2304]{1,0:T(8,128)} fusion(bf16[1152,768]{0,1:T(8,128)(2,1)} %fusion.16, bf16[768,2304]{1,0:T(8,128)(2,1)} %all-gather.6.cloned.1.call-done), kind=kOutput, calls=%fused_computation.105 | convolution fusion | flops 4076863488 | bytes 15925248 | tf_op jit(solution)/shard_map/dot_general | solution.py:300
  54.0 28.9 %attend.1 = (bf16[1152,768]{1,0:T(8,128)(2,1)S(1)}, bf16[1152,768]{1,0:T(8,128)(2,1)}, bf16[1152,768]{1,0:T(8,128)(2,1)}, bf16[1024,768]{1,0:T(8,128)(2,1)S(1)}, bf16[6,8,256,256]{3,2,1,0:T(8,128)(2,1)}) custom-call(s32[5]{0:T(128)S(1)} %pad_add_fusion.bounds, f32[1152,2304]{1,0:T(8,128)} %fusion.44.mq.mk.mv, f32[1152,2304]{1,0:T(8,128)} %fusion.44.mq.mk.mv, ...), custom_call_target="tpu_custom_call" | custom-call | tf_op jit(solution)/shard_map/attend/pallas_call | solution.py:184
  83.0 1.1 copy-done
  84.1 3.8 fusion.43
  87.9 1.7 copy-done.5
  90.0 4.5 all-gather.10.cloned.1.call-done
  94.5 10.6 %fusion.38 = f32[1024,2304]{1,0:T(8,128)} fusion(bf16[768,2304]{1,0:T(8,128)(2,1)} %all-gather.10.cloned.1.call-done, f32[1024,768]{0,1:T(8,128)} %copy-done.5, f32[768]{0:T(1024)S(1)} %get-tuple-element.92, f32[1024]{0:T(1024)S(1)} %add_rsqrt_fusion.2, f32[1024]{0:T(1024)S(1)} %broadcast_multiply_fusion.6), kind=kOutput, calls=%fused_computation.100 | convolution fusion | flops 3627024384 | bytes 16133120 | tf_op jit(solution)/shard_map/dot_general | solution.py:305
  105.1 11.6 %all-gather.12.cloned.1.call-done = bf16[1152,768]{1,0:T(8,128)(2,1)} async-done(((bf16[288,768]{1,0:T(8,128)(2,1)}), bf16[1152,768]{1,0:T(8,128)(2,1)}) %all-gather.12.cloned.1.call-update) | async-done | bytes 1769488 | tf_op jit(solution)/shard_map/all_gather | solution.py:275
  116.7 16.2 %add_convert_fusion = (bf16[1024,1152]{1,0:T(8,128)(2,1)S(1)}, f32[1024,1152]{1,0:T(8,128)S(1)}, f32[1024,1152]{1,0:T(8,128)S(1)}) fusion(f32[1024,2304]{1,0:T(8,128)} %fusion.38, bf16[1152,768]{1,0:T(8,128)(2,1)} %all-gather.12.cloned.1.call-done, bf16[1,1024,768]{2,1,0:T(8,128)(2,1)} %param.14), kind=kOutput, calls=%fused_computation.9 | convolution fusion | flops 1898053632 | bytes 24576000 | tf_op jit(solution)/shard_map/dot_general | solution.py:29
  133.0 2.6 multiply_convert_fusion
  135.6 1.1 copy-done.6
  136.6 6.4 %multiply_reduce_fusion = (f32[768]{0:T(1024)S(1)}, f32[1024]{0:T(1024)S(1)}, f32[1024]{0:T(1024)S(1)}, f32[1024,768]{0,1:T(8,128)S(1)}) fusion(f32[1024,768]{0,1:T(8,128)S(1)} %copy-done.6, f32[1024]{0:T(1024)S(1)} %add_rsqrt_fusion.2, f32[1024]{0:T(1024)S(1)} %broadcast_multiply_fusion.6, f32[768]{0:T(1024)S(1)} %get-tuple-element.92, ...), kind=kOutput, calls=%fused_computation.46 | convolution fusion | flops 3639604480 | bytes 14571520 | tf_op jit(solution)/shard_map/dot_general | solution.py:29
  143.1 1.0 multiply_add_fusion
  144.2 1.7 copy-done.7
  145.8 2.5 convolution_convert_fusion.4
  148.4 5.4 convolution_convert_fusion.2
  153.8 9.3 %convolution_convert_fusion = bf16[768,2304]{1,0:T(8,128)(2,1)} fusion(bf16[1024,1152]{1,0:T(8,128)(2,1)} %copy-done.10, bf16[1024,1152]{1,0:T(8,128)(2,1)} %copy-done.15, f32[1024,768]{0,1:T(8,128)} %copy-done.5, f32[768]{0:T(1024)S(1)} %get-tuple-element.92, f32[1024]{0:T(1024)S(1)} %add_rsqrt_fusion.2, f32[1024]{0:T(1024)S(1)} %broadcast_multiply_fusion.6), kind=kOutput, calls=%fused_computation.1 | convolution fusion | flops 3638231040 | bytes 11414528 | tf_op jit(solution)/shard_map/dot_general | solution.py:23
  163.3 3.9 convolution_convert_fusion.3.grad_context
  167.2 25.8 %attend_back.1 = (bf16[1024,2304]{1,0:T(8,128)(2,1)}, bf16[128,1536]{1,0:T(8,128)(2,1)S(1)}) custom-call(bf16[1152,768]{1,0:T(8,128)(2,1)S(1)} %get-tuple-element.40.query, bf16[1152,768]{1,0:T(8,128)(2,1)} %get-tuple-element.41.key, bf16[1152,768]{1,0:T(8,128)(2,1)} %get-tuple-element.42.value, bf16[6,8,256,256]{3,2,1,0:T(8,128)(2,1)} %get-tuple-element.43.probs, ...), custom_call_target="tpu_custom_call" | custom-call | tf_op jit(solution)/shard_map/attend_back/pallas_call | solution.py:218
  193.0 3.3 collective-permute-start.2
  196.9 0.6 and_reduce_fusion
  197.5 1.3 collective-permute-start.3
  198.8 2.0 collective-permute-done.2
  200.9 3.0 add_select_fusion
  203.9 4.1 scatter-add.6
  208.0 1.7 fusion.33
  209.7 8.6 %convolution_convert_fusion.1 = bf16[768,2304]{1,0:T(8,128)(2,1)} fusion(bf16[1024,2304]{1,0:T(8,128)(2,1)} %fusion.33, bf16[1152,768]{0,1:T(8,128)(2,1)} %fusion.16), kind=kOutput, calls=%fused_computation.2 | convolution fusion | flops 3625648128 | bytes 9830400 | tf_op jit(solution)/shard_map/dot_general | solution.py:23
  218.4 0.7 reduce-scatter.15.cloned.1.call-update
  219.2 1.8 pad.12
  221.8 27.4 %reduce-scatter.17.cloned.1.call-done = bf16[192,2304]{1,0:T(8,128)(2,1)} async-done(((bf16[768,2304]{1,0:T(8,128)(2,1)}), bf16[192,2304]{1,0:T(8,128)(2,1)}) %reduce-scatter.17.cloned.1.call-update) | async-done | bytes 884752 | tf_op jit(solution)/shard_map/reduce_scatter | solution.py:254
  249.4 5.4 fusion.30
  254.8 1.8 copy.69
  256.6 10.4 %fusion.22 = (f32[768]{0:T(1024)S(1)}, f32[1024]{0:T(1024)S(1)}, f32[1024]{0:T(1024)S(1)}, f32[1024,768]{0,1:T(8,128)}) fusion(f32[1024]{0:T(1024)S(1)} %add_rsqrt_fusion.1, f32[1024]{0:T(1024)S(1)} %broadcast_multiply_fusion.3, bf16[1,1024,768]{1,2,0:T(8,128)(2,1)S(1)} %copy-done.3, f32[768]{0:T(1024)S(1)} %get-tuple-element.93, ...), kind=kOutput, calls=%fused_computation.44 | convolution fusion | flops 3630953728 | bytes 12998656 | tf_op jit(solution)/shard_map/dot_general | solution.py:29
  266.9 25.5 %reduce-scatter.9.cloned.1.call-done = bf16[192,2304]{1,0:T(8,128)(2,1)} async-done(((bf16[768,2304]{1,0:T(8,128)(2,1)}), bf16[192,2304]{1,0:T(8,128)(2,1)}) %reduce-scatter.9.cloned.1.call-update) | async-done | bytes 884752 | tf_op jit(solution)/shard_map/reduce_scatter | solution.py:254
  292.5 3.9 fusion.25
  296.4 1.6 copy.70
  298.0 39.5 %psum.7 = f32[2,768]{1,0:T(2,128)S(1)} all-reduce(f32[2,768]{1,0:T(2,128)S(1)} %pad_maximum_fusion.3), channel_id=1, replica_groups=mesh['seq'=8,'fsdp'=4] {'seq','fsdp'}, use_global_device_ids=true, to_apply=%region_22.23 | all-reduce | flops 1536 | bytes 12288 | tf_op jit(solution)/shard_map/psum | solution.py:335
  337.5 0.6 fusion.41
  338.1 16.4 %reduce-scatter.15.cloned.1.call-done = bf16[24,768]{1,0:T(8,128)(2,1)} async-done(((bf16[192,768]{1,0:T(8,128)(2,1)}), bf16[24,768]{1,0:T(8,128)(2,1)}) %reduce-scatter.15.cloned.1.call-update) | async-done | bytes 36880 | tf_op jit(solution)/shard_map/reduce_scatter | solution.py:261
  354.6 31.4 %all_gather.33 = bf16[192,768]{1,0:T(8,128)(2,1)S(1)} all-gather(bf16[24,768]{1,0:T(8,128)(2,1)} %reduce-scatter.15.cloned.1.call-done), channel_id=1, replica_groups=mesh['seq'=8,'fsdp'=4] {'seq'}, dimensions={0}, use_global_device_ids=true | all-gather | bytes 331776 | tf_op jit(solution)/shard_map/all_gather | solution.py:262
  385.9 0.9 convert_element_type.82
  386.8 30.0 %reduce-scatter.23.cloned.1.call-done = bf16[40,768]{1,0:T(8,128)(2,1)} async-done(((bf16[320,768]{1,0:T(8,128)(2,1)}), bf16[40,768]{1,0:T(8,128)(2,1)}) %reduce-scatter.23.cloned.1.call-update) | async-done | bytes 61456 | tf_op jit(solution)/shard_map/reduce_scatter | solution.py:261
  416.8 31.7 %all_gather.35 = bf16[320,768]{1,0:T(8,128)(2,1)S(1)} all-gather(bf16[40,768]{1,0:T(8,128)(2,1)} %reduce-scatter.23.cloned.1.call-done), channel_id=1, replica_groups=mesh['seq'=8,'fsdp'=4] {'seq'}, dimensions={0}, use_global_device_ids=true | all-gather | bytes 552960 | tf_op jit(solution)/shard_map/all_gather | solution.py:262
  448.5 1.0 slice_convert_fusion
  449.5 31.0 %reduce-scatter.19.cloned.1.call-done = bf16[24,2304]{1,0:T(8,128)(2,1)} async-done(((bf16[192,2304]{1,0:T(8,128)(2,1)}), bf16[24,2304]{1,0:T(8,128)(2,1)}) %reduce-scatter.19.cloned.1.call-update) | async-done | bytes 110608 | tf_op jit(solution)/shard_map/reduce_scatter | solution.py:261
  480.5 33.4 %all_gather.34 = bf16[192,2304]{1,0:T(8,128)(2,1)S(1)} all-gather(bf16[24,2304]{1,0:T(8,128)(2,1)} %reduce-scatter.19.cloned.1.call-done), channel_id=1, replica_groups=mesh['seq'=8,'fsdp'=4] {'seq'}, dimensions={0}, use_global_device_ids=true | all-gather | bytes 995328 | tf_op jit(solution)/shard_map/all_gather | solution.py:262
  513.9 1.3 convert_element_type.84
  515.2 30.0 %reduce-scatter.11.cloned.1.call-done = bf16[24,2304]{1,0:T(8,128)(2,1)} async-done(((bf16[192,2304]{1,0:T(8,128)(2,1)}), bf16[24,2304]{1,0:T(8,128)(2,1)}) %reduce-scatter.11.cloned.1.call-update) | async-done | bytes 110608 | tf_op jit(solution)/shard_map/reduce_scatter | solution.py:261
  545.2 32.8 %all_gather.32 = bf16[192,2304]{1,0:T(8,128)(2,1)S(1)} all-gather(bf16[24,2304]{1,0:T(8,128)(2,1)} %reduce-scatter.11.cloned.1.call-done), channel_id=1, replica_groups=mesh['seq'=8,'fsdp'=4] {'seq'}, dimensions={0}, use_global_device_ids=true | all-gather | bytes 995328 | tf_op jit(solution)/shard_map/all_gather | solution.py:262
  578.0 1.3 convert_element_type.80
  (88 shorter events, 4.0 us)
Async XLA Ops:
  7.2 11.9 %copy-start.12 = (bf16[192]{0:T(256)(128)(2,1)S(1)}, bf16[192]{0:T(256)(128)(2,1)}, u32[]{:S(2)}) copy-start(bf16[192]{0:T(256)(128)(2,1)} %param.20) | copy-start | bytes 1156
  7.2 11.9 %copy-start.13 = (bf16[192]{0:T(256)(128)(2,1)S(1)}, bf16[192]{0:T(256)(128)(2,1)}, u32[]{:S(2)}) copy-start(bf16[192]{0:T(256)(128)(2,1)} %param.21) | copy-start | bytes 1156
  7.2 17.1 %copy-start.11 = (s32[1,3]{1,0:T(1,128)S(1)}, s32[1,3]{1,0:T(1,128)}, u32[]{:S(2)}) copy-start(s32[1,3]{1,0:T(1,128)} %param.15) | copy-start | bytes 40
  7.2 35.9 %all-gather.6.cloned.1.call-start = ((), (), s32[]{:S(2)}) async-start(), calls=%async_computation.8 | async-start | bytes 4423680 | tf_op jit(solution)/shard_map/all_gather | solution.py:272
  7.9 76.2 %all-gather.8.cloned.1.call-start = ((), (), s32[]{:S(2)}) async-start(), calls=%async_computation.9 | async-start | bytes 1474560 | tf_op jit(solution)/shard_map/all_gather | solution.py:273
  8.7 85.9 %all-gather.10.cloned.1.call-start = ((), (), s32[]{:S(2)}) async-start(), calls=%async_computation.10 | async-start | bytes 4423680 | tf_op jit(solution)/shard_map/all_gather | solution.py:274
  9.4 107.3 %all-gather.12.cloned.1.call-start = ((), (), s32[]{:S(2)}) async-start(), calls=%async_computation.11 | async-start | bytes 2211840 | tf_op jit(solution)/shard_map/all_gather | solution.py:275
  11.2 17.1 %copy-start.2 = (bf16[1,1024,768]{1,2,0:T(8,128)(2,1)}, bf16[1,1024,768]{1,2,0:T(8,128)(2,1)S(1)}, u32[]{:S(2)}) copy-start(bf16[1,1024,768]{1,2,0:T(8,128)(2,1)S(1)} %copy.59) | copy-start | bytes 4718596
  12.1 16.1 %collective-permute-start = (bf16[64,768]{0,1:T(8,128)(2,1)}, bf16[64,768]{0,1:T(8,128)(2,1)}, u32[]{:S(2)}, u32[]{:S(2)}) collective-permute-start(bf16[64,768]{0,1:T(8,128)(2,1)} %get-tuple-element.99), channel_id=1, source_target_pairs={{0,4},{4,8},{8,12},{12,16},{16,20},{20,24},{24,28},{1,5},{5,9},{9,... | collective-permute-start | bytes 294920 | tf_op jit(solution)/shard_map/ppermute | solution.py:250
  17.6 10.6 %collective-permute-start.1 = (bf16[64,768]{0,1:T(8,128)(2,1)}, bf16[64,768]{0,1:T(8,128)(2,1)}, u32[]{:S(2)}, u32[]{:S(2)}) collective-permute-start(bf16[64,768]{0,1:T(8,128)(2,1)} %get-tuple-element.98), channel_id=1, source_target_pairs={{4,0},{8,4},{12,8},{16,12},{20,16},{24,20},{28,24},{5,1},{9,5},{13... | collective-permute-start | bytes 294920 | tf_op jit(solution)/shard_map/ppermute | solution.py:250
  19.0 199.5 %reduce-scatter.13.cloned.1.call-start = ((), (), s32[]{:S(2)}) async-start(), calls=%async_computation.14 | async-start | bytes 1474560 | tf_op jit(solution)/shard_map/reduce_scatter | solution.py:254
  32.2 3.9 copy-start.4
  83.0 1.1 copy-start
  87.9 1.7 copy-start.5
  116.7 16.2 %copy-start.8 = (f32[1024,2304]{1,0:T(8,128)S(1)}, f32[1024,2304]{1,0:T(8,128)}, u32[]{:S(2)}) copy-start(f32[1024,2304]{1,0:T(8,128)} %fusion.38) | copy-start | bytes 28311556
  132.9 2.6 copy-start.15
  132.9 3.7 copy-start.6
  135.5 7.5 %copy-start.10 = (bf16[1024,1152]{1,0:T(8,128)(2,1)}, bf16[1024,1152]{1,0:T(8,128)(2,1)S(1)}, u32[]{:S(2)}) copy-start(bf16[1024,1152]{1,0:T(8,128)(2,1)S(1)} %get-tuple-element.96) | copy-start | bytes 7077892
  136.6 6.5 %copy-start.9 = (bf16[1,1024,768]{1,2,0:T(8,128)(2,1)S(1)}, bf16[1,1024,768]{1,2,0:T(8,128)(2,1)}, u32[]{:S(2)}) copy-start(bf16[1,1024,768]{1,2,0:T(8,128)(2,1)} %copy.66) | copy-start | bytes 4718596
  143.1 2.7 copy-start.1
  144.1 1.7 copy-start.7
  148.3 70.8 %reduce-scatter.21.cloned.1.call-start = ((), (), s32[]{:S(2)}) async-start(), calls=%async_computation.18 | async-start | bytes 2211840 | tf_op jit(solution)/shard_map/reduce_scatter | solution.py:254
  153.8 95.5 %reduce-scatter.17.cloned.1.call-start = ((), (), s32[]{:S(2)}) async-start(), calls=%async_computation.16 | async-start | bytes 4423680 | tf_op jit(solution)/shard_map/reduce_scatter | solution.py:254
  163.2 129.3 %reduce-scatter.9.cloned.1.call-start = ((), (), s32[]{:S(2)}) async-start(), calls=%async_computation.12 | async-start | bytes 4423680 | tf_op jit(solution)/shard_map/reduce_scatter | solution.py:254
  167.1 29.8 %copy-start.14 = (s32[2]{0:T(128)S(1)}, s32[2]{0:T(128)}, u32[]{:S(2)}) copy-start(s32[2]{0:T(128)} %constant.155.clone.1) | copy-start | bytes 28
  193.0 7.8 %collective-permute-start.2 = (bf16[64,1536]{1,0:T(8,128)(2,1)S(1)}, bf16[64,1536]{1,0:T(8,128)(2,1)S(1)}, u32[]{:S(2)}, u32[]{:S(2)}) collective-permute-start(bf16[64,1536]{1,0:T(8,128)(2,1)S(1)} %get-tuple-element.101), channel_id=1, source_target_pairs={{0,4},{4,8},{8,12},{12,16},{16,20},{20,24},{24,28},{1,5},{5,9},{9,... | collective-permute-start | bytes 589832 | tf_op jit(solution)/shard_map/ppermute | solution.py:250
  197.5 10.5 %collective-permute-start.3 = (bf16[64,1536]{1,0:T(8,128)(2,1)S(1)}, bf16[64,1536]{1,0:T(8,128)(2,1)S(1)}, u32[]{:S(2)}, u32[]{:S(2)}) collective-permute-start(bf16[64,1536]{1,0:T(8,128)(2,1)S(1)} %get-tuple-element.100), channel_id=1, source_target_pairs={{4,0},{8,4},{12,8},{16,12},{20,16},{24,20},{28,24},{5,1},{9,5},{13... | collective-permute-start | bytes 589832 | tf_op jit(solution)/shard_map/ppermute | solution.py:250
  218.3 2.8 copy-start.3
  218.3 136.2 %reduce-scatter.15.cloned.1.call-start = ((), (), s32[]{:S(2)}) async-start(), calls=%async_computation.15 | async-start | bytes 331776 | tf_op jit(solution)/shard_map/reduce_scatter | solution.py:261
  219.1 197.8 %reduce-scatter.23.cloned.1.call-start = ((), (), s32[]{:S(2)}) async-start(), calls=%async_computation.19 | async-start | bytes 552960 | tf_op jit(solution)/shard_map/reduce_scatter | solution.py:261
  221.0 259.5 %reduce-scatter.19.cloned.1.call-start = ((), (), s32[]{:S(2)}) async-start(), calls=%async_computation.17 | async-start | bytes 995328 | tf_op jit(solution)/shard_map/reduce_scatter | solution.py:261
  249.3 295.9 %reduce-scatter.11.cloned.1.call-start = ((), (), s32[]{:S(2)}) async-start(), calls=%async_computation.13 | async-start | bytes 995328 | tf_op jit(solution)/shard_map/reduce_scatter | solution.py:261
Sparse Core Ops, SparseCore 0:
  9.6 33.4 all-gather.5
  44.7 17.4 all-gather.7
  63.7 30.7 all-gather.9
  96.0 20.7 all-gather.11
  148.5 25.7 reduce-scatter.12
  176.8 29.4 reduce-scatter.20
  208.8 40.3 reduce-scatter.16
  252.0 40.4 reduce-scatter.8
  295.8 58.7 reduce-scatter.14
  358.3 58.4 reduce-scatter.22
  420.3 60.1 reduce-scatter.18
  483.7 61.4 reduce-scatter.10
